TPU v7x, 32 devices: a whole 2x2x4 slice. The times are simulated.
32 devices in a mesh: groups: 2 (over x), tensor: 8 (over z, y), examples: 2 (over core).
Axes of the slice: x: 2, y: 2, z: 4, core: 2. Of those that a mesh axis runs over, the one named last changes fastest.
Arguments:
- act_up: bfloat16 [64, 16, 8192], P(('groups', 'examples'), None, 'tensor'), parts along dimension 0, may hold values from -6 to 6
- grad_up: bfloat16 [64, 16, 28672], P(('groups', 'examples'), None, 'tensor'), parts along dimension 0, may hold values from -6 to 6
- act_down: bfloat16 [64, 16, 28672], P(('groups', 'examples'), None, 'tensor'), parts along dimension 0, may hold values from -6 to 6
- grad_down: bfloat16 [64, 16, 8192], P(('groups', 'examples'), None, 'tensor'), parts along dimension 0, may hold values from -6 to 6
- basis_act_up: bfloat16 [8192, 64], P('tensor'), may hold values from -0.0625 to 0.0625
- basis_grad_up: bfloat16 [28672, 128], P('tensor'), may hold values from -0.03125 to 0.03125
- basis_act_down: bfloat16 [28672, 64], P('tensor'), may hold values from -0.03125 to 0.03125
- basis_grad_down: bfloat16 [8192, 128], P('tensor'), may hold values from -0.0625 to 0.0625
Outputs:
- feature_up: float32 [4, 16, 8192], P(('groups', 'examples'), 'tensor'), parts along dimension 0
- gram_up: float32 [16384, 8192], P(('groups', 'examples'), 'tensor'), parts along dimension 0
- feature_down: float32 [4, 16, 8192], P(('groups', 'examples'), 'tensor'), parts along dimension 0
- gram_down: float32 [16384, 8192], P(('groups', 'examples'), 'tensor'), parts along dimension 0
There are 2 independent parts, one for each index of `groups`. A program takes and returns all parts, laid end to end along the dimension named above; an argument that names none is the same for every part. Nothing has to cross between parts.
All inputs are finite; a program needn't handle non-finite values.
Results may differ from a plain program's by a relative error of at most 0.0003.
Values sent between devices are 32-bit elements; how exact they have to be, the bound alone decides.
A program may use at most 128 MiB of HBM per device.

v0:
```python
import math

import jax
import jax.numpy as jnp
from jax import lax
from jax.sharding import PartitionSpec as P


def project_rows(pairs):
    pieces = [jnp.dot(acts, basis, preferred_element_type=jnp.float32) for acts, basis in pairs]
    return jnp.concatenate(pieces, axis=1)


def outer_features(proj_act, proj_grad, seq_len):
    owned = proj_act.shape[0] // seq_len
    act_part = proj_act.reshape(owned, seq_len, proj_act.shape[1])
    grad_part = proj_grad.reshape(owned, seq_len, proj_grad.shape[1])
    summed = jnp.einsum("bsa,bsc->bac", grad_part, act_part, precision=lax.Precision.HIGHEST)
    summed = summed / math.sqrt(seq_len)
    return summed.reshape(owned, summed.shape[1] * summed.shape[2])


def cross_product(left, right):
    return lax.dot_general(
        left,
        right,
        (((0,), (0,)), ((), ())),
        precision=lax.Precision.HIGHEST,
        preferred_element_type=jnp.float32,
    )


def shards(
    act_up,
    grad_up,
    act_down,
    grad_down,
    basis_act_up,
    basis_grad_up,
    basis_act_down,
    basis_grad_down,
):
    ex_local, seq_len = (act_up.shape[0], act_up.shape[1])
    token_rows = ex_local * seq_len
    pairs = (
        (act_up.reshape(token_rows, act_up.shape[2]), basis_act_up),
        (grad_up.reshape(token_rows, grad_up.shape[2]), basis_grad_up),
        (act_down.reshape(token_rows, act_down.shape[2]), basis_act_down),
        (grad_down.reshape(token_rows, grad_down.shape[2]), basis_grad_down),
    )
    owned = lax.psum_scatter(project_rows(pairs), "tensor", scatter_dimension=0, tiled=True)
    width_in = basis_act_up.shape[1]
    width_out = basis_grad_up.shape[1]
    first_cut = width_in + width_out
    feature_one = outer_features(owned[:, :width_in], owned[:, width_in:first_cut], seq_len)
    feature_two = outer_features(
        owned[:, first_cut : first_cut + width_in], owned[:, first_cut + width_in :], seq_len
    )
    owned_examples = feature_one.shape[0]
    feat_width = feature_one.shape[1]
    col_width = feat_width // lax.axis_size("tensor")
    col_start = lax.axis_index("tensor") * col_width
    row_width = feat_width // lax.axis_size("examples")
    gathered = (
        lax.all_gather(feature_one, ("tensor", "examples"), axis=0, tiled=True),
        lax.all_gather(feature_two, ("tensor", "examples"), axis=0, tiled=True),
    )
    total_examples = gathered[0].shape[0]
    row_start = lax.axis_index("examples") * row_width
    blocks = [
        cross_product(
            lax.dynamic_slice_in_dim(whole, row_start, row_width, 1),
            lax.dynamic_slice_in_dim(whole, col_start, col_width, 1),
        )
        / total_examples
        for whole in gathered
    ]
    gram_one = blocks[0]
    gram_two = blocks[1]
    return (
        feature_one.reshape(1, owned_examples, feat_width),
        gram_one,
        feature_two.reshape(1, owned_examples, feat_width),
        gram_two,
    )


def solution(mesh):
    in_specs = (
        P(("groups", "examples"), None, "tensor"),
        P(("groups", "examples"), None, "tensor"),
        P(("groups", "examples"), None, "tensor"),
        P(("groups", "examples"), None, "tensor"),
        P("tensor", None),
        P("tensor", None),
        P("tensor", None),
        P("tensor", None),
    )
    out_specs = (
        P(("groups", "examples"), "tensor", None),
        P(("groups", "examples"), "tensor"),
        P(("groups", "examples"), "tensor", None),
        P(("groups", "examples"), "tensor"),
    )
    return jax.shard_map(shards, mesh=mesh, in_specs=in_specs, out_specs=out_specs, check_vma=False)
```

profile of v0, /device:TPU:1, one launch (start us, length us, event | category | flops | bytes accessed | tf_op | source)
XLA Modules:
  0.0 183.3 jit_solution(9943071226701789212)
XLA Ops:
  7.2 0.0 reduce-scatter.4.cloned.1.call-start
  7.2 1.5 fusion.8
  8.7 2.2 %fusion.10 = f32[256,64]{0,1:T(8,128)S(1)} fusion(bf16[256,3584]{1,0:T(8,128)(2,1)} %bitcast.22, bf16[3584,64]{0,1:T(8,128)(2,1)} %param.14), kind=kOutput, calls=%fused_computation.15 | convolution fusion | flops 117440512 | bytes 2359296 | tf_op jit(solution)/shard_map/dot_general | solution.py:10
  11.0 1.9 %fusion.9 = f32[256,128]{0,1:T(8,128)S(1)} fusion(bf16[256,3584]{1,0:T(8,128)(2,1)S(1)} %bitcast.21, bf16[3584,128]{1,0:T(8,128)(2,1)} %param.13), kind=kOutput, calls=%fused_computation.14 | convolution fusion | flops 234881024 | bytes 2883584 | tf_op jit(solution)/shard_map/dot_general | solution.py:10
  12.9 1.4 fusion.11
  14.3 0.9 copy.28
  15.3 0.0 reduce-scatter.4.cloned.1.call-update
  15.3 0.0 all-gather.5.cloned.1.call-start
  15.3 61.7 %reduce-scatter.4.cloned.1.call-done = f32[32,384]{1,0:T(8,128)} async-done(((f32[256,384]{1,0:T(8,128)}), f32[32,384]{1,0:T(8,128)}) %reduce-scatter.4.cloned.1.call-update) | async-done | bytes 49168 | tf_op jit(solution)/shard_map/reduce_scatter | solution.py:51
  77.0 0.8 fusion.7
  77.8 0.8 fusion.6
  78.7 0.3 convolution_multiply_fusion.3
  79.0 0.1 copy.24
  79.1 0.7 reshape_reshape.6
  79.8 0.0 all-gather.7.cloned.1.call-start
  79.9 0.3 convolution_multiply_fusion.2
  80.2 0.1 copy.27
  80.3 0.7 reshape_reshape.7
  81.0 38.2 %all-gather.5.cloned.1.call-done = f32[16,2,8192]{2,1,0:T(2,128)} async-done(((f32[1,2,8192]{2,1,0:T(2,128)}), f32[16,2,8192]{2,1,0:T(2,128)}) %all-gather.5.cloned.1.call-update) | async-done | bytes 1048592 | tf_op jit(solution)/shard_map/all_gather | solution.py:65
  119.2 1.9 %reshape.49 = f32[32,8192]{1,0:T(8,128)S(1)} reshape(f32[16,2,8192]{2,1,0:T(2,128)} %all-gather.5.cloned.1.call-done) | data formatting | bytes 2097152
  121.2 16.0 %convolution_multiply_fusion.1 = f32[4096,1024]{1,0:T(8,128)} fusion(f32[32,8192]{1,0:T(8,128)S(1)} %reshape.49, s32[]{:T(128)S(6)} %select_n.8, s32[]{:T(128)S(6)} %select_n.9), kind=kOutput, calls=%fused_computation.1 | convolution fusion | flops 1614807040 | bytes 17432584 | tf_op jit(solution)/shard_map/dot_general | solution.py:24
  137.2 21.7 %all-gather.7.cloned.1.call-done = f32[16,2,8192]{2,1,0:T(2,128)} async-done(((f32[1,2,8192]{2,1,0:T(2,128)}), f32[16,2,8192]{2,1,0:T(2,128)}) %all-gather.7.cloned.1.call-update) | async-done | bytes 1048592 | tf_op jit(solution)/shard_map/all_gather | solution.py:66
  158.9 1.9 %reshape.51 = f32[32,8192]{1,0:T(8,128)S(1)} reshape(f32[16,2,8192]{2,1,0:T(2,128)} %all-gather.7.cloned.1.call-done) | data formatting | bytes 2097152
  160.8 16.0 %convolution_multiply_fusion = f32[4096,1024]{1,0:T(8,128)} fusion(f32[32,8192]{1,0:T(8,128)S(1)} %reshape.51, s32[]{:T(128)S(6)} %select_n.8, s32[]{:T(128)S(6)} %select_n.9), kind=kOutput, calls=%fused_computation | convolution fusion | flops 1614807040 | bytes 17432584 | tf_op jit(solution)/shard_map/dot_general | solution.py:24
  (5 shorter events, 0.1 us)
Async XLA Ops:
  7.2 3.8 %copy-start = (bf16[16,16,3584]{2,1,0:T(8,128)(2,1)S(1)}, bf16[16,16,3584]{2,1,0:T(8,128)(2,1)}, u32[]{:S(2)}) copy-start(bf16[16,16,3584]{2,1,0:T(8,128)(2,1)} %param.9) | copy-start | bytes 5505028
  7.2 69.8 %reduce-scatter.4.cloned.1.call-start = ((), (), s32[]{:S(2)}) async-start(), calls=%async_computation.3 | async-start | bytes 442368 | tf_op jit(solution)/shard_map/reduce_scatter | solution.py:51
  15.3 104.0 %all-gather.5.cloned.1.call-start = ((), (), s32[]{:S(2)}) async-start(), calls=%async_computation.1 | async-start | bytes 1114112 | tf_op jit(solution)/shard_map/all_gather | solution.py:65
  79.8 79.1 %all-gather.7.cloned.1.call-start = ((), (), s32[]{:S(2)}) async-start(), calls=%async_computation.2 | async-start | bytes 1114112 | tf_op jit(solution)/shard_map/all_gather | solution.py:66
Sparse Core Ops, SparseCore 0:
  15.4 61.5 reduce-scatter.3
  79.9 39.2 all-gather.4
  122.0 36.8 all-gather.6
where the time goes:
time: 184 us; the launch traced here: 183 us
  waiting for transfers between devices  122 us (66%)
  matrix products  39.6 us (22%)
  between operations  13.8 us (8%)
  local copies, waits for them, and re-layouts  8.14 us (4%)
    reduce_scatter x1, waiting for transfers between devices, shards(): lax.psum_scatter(project_rows(pairs), 'tensor', scatter_dimension=0, tile...  61.7 us
    all_gather x1, waiting for transfers between devices, shards(): lax.all_gather(feature_one, ('tensor', 'examples'), axis=0, tiled=True)  38.2 us
    dot_general x2, matrix products, cross_product(): lax.dot_general(left, right, (((0,), (0,)), ((), ())), precision=lax.Prec...  32 us
    all_gather x1, waiting for transfers between devices, shards(): lax.all_gather(feature_two, ('tensor', 'examples'), axis=0, tiled=True)  21.7 us
    dot_general x4, matrix products, project_rows(): jnp.dot(acts, basis, preferred_element_type=jnp.float32)  7.06 us
    unnamed x5, local copies, waits for them, and re-layouts  4.81 us
  transfers between devices with their start and end apart: 3, of which 3 were waited for; matrix products, arithmetic and copies ran while one was open for 10% of the time, Pallas kernels for 0%

commit v1 on v0

v1 whole, which is shorter than its diff:
```python
import functools
import math

import jax
import jax.numpy as jnp
from jax import lax
from jax.experimental import pallas as pl
from jax.experimental.pallas import tpu as pltpu
from jax.sharding import PartitionSpec as P

LANES = 128
MESH = pl.DeviceIdType.MESH
VMEM_LIMIT = 56 * 1024 * 1024


def exchange_kernel(n_tensor, n_core, own_rows, act_up, grad_up, act_down, grad_down, b_au, b_gu, b_ad, b_gd,
                    gathered, v_au, v_gu, v_ad, v_gd, w_au, w_gu, w_ad, w_gd,
                    part, pair_in, line_in, whole, load_sem, out_sem,
                    pair_send, pair_recv, line_send, line_recv, gat_send, gat_recv,
                    back_send, back_recv, core_send, core_recv):
    n_line = n_tensor // 2
    t = lax.axis_index("tensor")
    e = lax.axis_index("examples")
    z, y = t // 2, t % 2
    pair = {"tensor": z * 2 + 1 - y}

    def line(step):
        return {"tensor": lax.rem(z + step, n_line) * 2 + y}

    sources = ((grad_down, b_gd, v_gd, w_gd), (grad_up, b_gu, v_gu, w_gu),
               (act_up, b_au, v_au, w_au), (act_down, b_ad, v_ad, w_ad))
    loads = []
    for i, (act, basis, v, w) in enumerate(sources):
        one = pltpu.make_async_copy(act, v, load_sem.at[2 * i])
        two = pltpu.make_async_copy(basis, w, load_sem.at[2 * i + 1])
        one.start()
        two.start()
        loads.append((one, two))

    barrier = pltpu.get_barrier_semaphore()
    pl.semaphore_signal(barrier, inc=1, device_id=pair, device_id_type=MESH)
    for step in range(1, n_line):
        pl.semaphore_signal(barrier, inc=1, device_id=line(step), device_id_type=MESH)
    for step in range(1, n_core):
        pl.semaphore_signal(barrier, inc=1, device_id={"examples": lax.rem(e + step, n_core)}, device_id_type=MESH)

    def product(i):
        loads[i][0].wait()
        loads[i][1].wait()
        v, w = sources[i][2:]
        return jnp.dot(v[...], w[...], preferred_element_type=jnp.float32)

    pair_copies = []
    for c in range(3):
        value = product(c) if c < 2 else jnp.concatenate([product(2), product(3)], axis=1)
        for owner in range(n_tensor):
            part[c, owner % 2, owner // 2] = value[owner * own_rows:(owner + 1) * own_rows]
        if c == 0:
            pl.semaphore_wait(barrier, 1 + (n_line - 1) + (n_core - 1))
        copy = pltpu.make_async_remote_copy(
            src_ref=part.at[c, 1 - y], dst_ref=pair_in.at[c], send_sem=pair_send.at[c], recv_sem=pair_recv.at[c],
            device_id=pair, device_id_type=MESH)
        copy.start()
        pair_copies.append(copy)

    line_copies = []
    for c in range(3):
        pair_copies[c].wait_recv()
        pair_in[c] = pair_in[c] + part[c, y]
        copies = []
        for step in range(1, n_line):
            copy = pltpu.make_async_remote_copy(
                src_ref=pair_in.at[c, lax.rem(z + step, n_line)], dst_ref=line_in.at[c, step - 1],
                send_sem=line_send.at[c, step - 1], recv_sem=line_recv.at[c, step - 1],
                device_id=line(step), device_id_type=MESH)
            copy.start()
            copies.append(copy)
        line_copies.append(copies)

    gat_copies = []
    for c in range(3):
        total = pair_in[c, z]
        for step in range(1, n_line):
            line_copies[c][step - 1].wait_recv()
            total = total + line_in[c, step - 1]
        whole[c, e, y, z] = total
        copies = []
        for step in range(1, n_line):
            copy = pltpu.make_async_remote_copy(
                src_ref=whole.at[c, e, y, z], dst_ref=whole.at[c, e, y, z],
                send_sem=gat_send.at[c, step - 1], recv_sem=gat_recv.at[c, step - 1],
                device_id=line(step), device_id_type=MESH)
            copy.start()
            copies.append(copy)
        gat_copies.append(copies)

    back_copies, core_copies, outs = [], [], []

    def to_cores(c, side, half):
        for step in range(1, n_core):
            copy = pltpu.make_async_remote_copy(
                src_ref=whole.at[c, e, half], dst_ref=whole.at[c, e, half],
                send_sem=core_send.at[c, side, step - 1], recv_sem=core_recv.at[c, side, step - 1],
                device_id={"examples": lax.rem(e + step, n_core)}, device_id_type=MESH)
            copy.start()
            core_copies.append(copy)

    for c in range(3):
        for copy in gat_copies[c]:
            copy.wait_recv()
        copy = pltpu.make_async_remote_copy(
            src_ref=whole.at[c, e, y], dst_ref=whole.at[c, e, y], send_sem=back_send.at[c], recv_sem=back_recv.at[c],
            device_id=pair, device_id_type=MESH)
        copy.start()
        back_copies.append(copy)
        to_cores(c, 0, y)
    for c in range(3):
        back_copies[c].wait_recv()
        to_cores(c, 1, 1 - y)
    for copy in core_copies:
        copy.wait_recv()
    out = pltpu.make_async_copy(whole, gathered, out_sem)
    out.start()
    out.wait()
    for copies in [pair_copies, back_copies, core_copies] + line_copies + gat_copies:
        for copy in copies:
            copy.wait_send()


def split_lanes(value):
    high = value.astype(jnp.bfloat16)
    low = (value - high.astype(jnp.float32)).astype(jnp.bfloat16)
    return high, low


def features_of(grad_pair, act_tile, first, columns, seq_len, width_in):
    width_out = grad_pair.shape[1] // 2
    batch = grad_pair.shape[0] // seq_len
    pick = lax.broadcasted_iota(jnp.int32, (width_out, columns), 0) - lax.broadcasted_iota(
        jnp.int32, (width_out, columns), 1) // width_in
    pick = jnp.where(pick == first, 1.0, 0.0).astype(jnp.bfloat16)
    pick = jnp.concatenate([pick, pick], axis=0)
    spread = jnp.dot(grad_pair, pick, preferred_element_type=jnp.float32)
    pieces = []
    for start in range(0, columns, LANES):
        piece = spread[:, start:start + LANES] * act_tile
        pieces.append(piece.reshape(seq_len, batch, LANES).sum(axis=0))
    return jnp.concatenate(pieces, axis=1)


def gram_kernel(n_tensor, n_core, seq_len, width_in, block, slots,
                gathered, feat_up, gram_up, feat_down, gram_down,
                rows, grad_pair, act_tile, own_grad, own_act, right, own_feat, held, load_sem, feat_sem, gram_sem):
    t = lax.axis_index("tensor")
    e = lax.axis_index("examples")
    n_line = n_tensor // 2
    batch = gathered.shape[1] // seq_len
    width_out = gathered.shape[2]
    own = own_grad.shape[0] // seq_len
    total_examples = batch
    a_rows = width_out // n_core
    a_cols = width_out // n_tensor
    a_block = block // width_in
    n_blocks = a_rows // a_block
    feat_part = own_feat.shape[2] // n_blocks
    a_part = feat_part // width_in
    own_at = pl.multiple_of((e * n_tensor + (t % 2) * n_line + t // 2) * (own * seq_len), own * seq_len)
    scale = 1.0 / math.sqrt(seq_len)

    load = pltpu.make_async_copy(gathered, rows, load_sem)
    load.start()
    load.wait()

    for layer, (gram, feat) in enumerate(((gram_up, feat_up), (gram_down, feat_down))):
        chunk = 1 - layer
        lane = lax.broadcasted_iota(jnp.int32, (batch, LANES), 1)
        for s in range(seq_len):
            at = pl.ds(s * batch, batch)
            high, low = split_lanes(rows[chunk, pl.ds(s, batch, seq_len), :])
            grad_pair[at, :width_out] = high
            grad_pair[at, width_out:] = low
            act = rows[2, pl.ds(s, batch, seq_len), :] * scale
            turned = pltpu.roll(act, width_in, axis=1)
            first, second = (act, turned) if layer == 0 else (turned, act)
            act_tile[at, :] = jnp.where(lane < width_in, first, second)
        lane = lax.broadcasted_iota(jnp.int32, (own, LANES), 1)
        grads, acts = [], []
        for s in range(seq_len):
            grads.append(rows[chunk, pl.ds(own_at + s, own, seq_len), :])
            act = rows[2, pl.ds(own_at + s, own, seq_len), :] * scale
            turned = pltpu.roll(act, width_in, axis=1)
            first, second = (act, turned) if layer == 0 else (turned, act)
            acts.append(jnp.where(lane < width_in, first, second))
        high, low = split_lanes(jnp.concatenate(grads, axis=0))
        own_grad[:, :width_out] = high
        own_grad[:, width_out:] = low
        own_act[...] = jnp.concatenate(acts, axis=0)

        columns = a_cols * width_in
        value = features_of(grad_pair[...], act_tile[...], t * a_cols, columns, seq_len, width_in)
        high, low = split_lanes(value * (1.0 / total_examples))
        right[0:batch] = high
        right[batch:2 * batch] = low
        right[2 * batch:] = high

        def step(i, carry):
            slot = lax.rem(i + layer * n_blocks, slots)
            value = features_of(grad_pair[...], act_tile[...], e * a_rows + i * a_block, block, seq_len, width_in)
            high, low = split_lanes(value)
            left = jnp.concatenate([high, high, low], axis=0)
            product = lax.dot_general(left, right[...], (((0,), (0,)), ((), ())), preferred_element_type=jnp.float32)

            def wait():
                pltpu.make_async_copy(held.at[slot], gram.at[pl.ds(0, block)], gram_sem.at[slot]).wait()

            if layer == 0:
                pl.when(i >= slots)(wait)
            else:
                wait()
            held[slot] = product
            pltpu.make_async_copy(
                held.at[slot], gram.at[pl.ds(pl.multiple_of(i * block, block), block)], gram_sem.at[slot]).start()
            value = features_of(own_grad[...], own_act[...], i * a_part, feat_part, seq_len, width_in)
            own_feat[layer, :, pl.ds(pl.multiple_of(i * feat_part, feat_part), feat_part)] = value
            return carry

        lax.fori_loop(0, n_blocks, step, 0)
        pltpu.make_async_copy(own_feat.at[layer], feat, feat_sem.at[layer]).start()

    for slot in range(slots):
        pltpu.make_async_copy(held.at[slot], gram_down.at[pl.ds(0, block)], gram_sem.at[slot]).wait()
    for layer, feat in enumerate((feat_up, feat_down)):
        pltpu.make_async_copy(own_feat.at[layer], feat, feat_sem.at[layer]).wait()


def shards(n_tensor, n_core, act_up, grad_up, act_down, grad_down, b_au, b_gu, b_ad, b_gd):
    ex_local, seq_len = act_up.shape[0], act_up.shape[1]
    token_rows = ex_local * seq_len
    acts = [a.reshape(token_rows, a.shape[2]) for a in (act_up, grad_up, act_down, grad_down)]
    bases = [b_au, b_gu, b_ad, b_gd]
    width_in, width_out = b_au.shape[1], b_gu.shape[1]
    own_rows = token_rows // n_tensor
    owned = own_rows // seq_len
    n_line = n_tensor // 2
    f32 = jnp.float32
    any_space = pl.BlockSpec(memory_space=pl.ANY)
    dma = pltpu.SemaphoreType.DMA
    steps = max(n_line - 1, 1)
    gathered = pl.pallas_call(
        functools.partial(exchange_kernel, n_tensor, n_core, own_rows),
        out_shape=jax.ShapeDtypeStruct((3, n_core, 2, n_line, own_rows, LANES), f32),
        in_specs=[any_space] * 8,
        out_specs=any_space,
        scratch_shapes=[pltpu.VMEM(a.shape, a.dtype) for a in acts + bases] + [
            pltpu.VMEM((3, 2, n_line, own_rows, LANES), f32),
            pltpu.VMEM((3, n_line, own_rows, LANES), f32),
            pltpu.VMEM((3, steps, own_rows, LANES), f32),
            pltpu.VMEM((3, n_core, 2, n_line, own_rows, LANES), f32),
            dma((8,)), dma,
            dma((3,)), dma((3,)), dma((3, steps)), dma((3, steps)), dma((3, steps)), dma((3, steps)),
            dma((3,)), dma((3,)), dma((3, 2, n_core - 1)), dma((3, 2, n_core - 1)),
        ],
        compiler_params=pltpu.CompilerParams(
            collective_id=0, has_side_effects=True, vmem_limit_bytes=VMEM_LIMIT),
        name="project_and_gather",
    )(*acts, *bases)

    tokens = n_core * token_rows
    batch = tokens // seq_len
    feat = width_in * width_out
    row_width, col_width = feat // n_core, feat // n_tensor
    block, slots = 512, 4
    shape = jax.ShapeDtypeStruct
    bf16 = jnp.bfloat16
    feature_one, gram_one, feature_two, gram_two = pl.pallas_call(
        functools.partial(gram_kernel, n_tensor, n_core, seq_len, width_in, block, slots),
        out_shape=[shape((owned, feat), f32), shape((row_width, col_width), f32)] * 2,
        in_specs=[any_space],
        out_specs=[any_space] * 4,
        scratch_shapes=[
            pltpu.VMEM((3, tokens, LANES), f32),
            pltpu.VMEM((tokens, 2 * width_out), bf16),
            pltpu.VMEM((tokens, LANES), f32),
            pltpu.VMEM((own_rows, 2 * width_out), bf16),
            pltpu.VMEM((own_rows, LANES), f32),
            pltpu.VMEM((3 * batch, col_width), bf16),
            pltpu.VMEM((2, owned, feat), f32),
            pltpu.VMEM((slots, block, col_width), f32),
            dma, dma((2,)), dma((slots,)),
        ],
        compiler_params=pltpu.CompilerParams(vmem_limit_bytes=VMEM_LIMIT),
        name="features_and_gram",
    )(gathered.reshape(3, tokens, LANES))
    return (
        feature_one.reshape(1, owned, feat),
        gram_one,
        feature_two.reshape(1, owned, feat),
        gram_two,
    )


def solution(mesh):
    in_specs = (
        P(("groups", "examples"), None, "tensor"),
        P(("groups", "examples"), None, "tensor"),
        P(("groups", "examples"), None, "tensor"),
        P(("groups", "examples"), None, "tensor"),
        P("tensor", None),
        P("tensor", None),
        P("tensor", None),
        P("tensor", None),
    )
    out_specs = (
        P(("groups", "examples"), "tensor", None),
        P(("groups", "examples"), "tensor"),
        P(("groups", "examples"), "tensor", None),
        P(("groups", "examples"), "tensor"),
    )
    body = functools.partial(shards, mesh.shape["tensor"], mesh.shape["examples"])
    return jax.shard_map(body, mesh=mesh, in_specs=in_specs, out_specs=out_specs, check_vma=False)
```

time: 184 us -> 49.7 us (0.27)
  waiting for transfers between devices: 122 us -> 0 us
  Pallas kernels: 0 us -> 44.8 us
  matrix products: 39.6 us -> 0 us
  between operations: 13.8 us -> 0.64 us
  local copies, waits for them, and re-layouts: 8.14 us -> 4 us
    reduce_scatter x1 -> x0, waiting for transfers between devices: 61.7 us -> none  [shards(): lax.psum_scatter(project_rows(pairs), 'tensor', scatter_dimension=0, tile...]
    all_gather x2 -> x0, waiting for transfers between devices: 59.9 us -> none  [the longest x1 38.2 us: shards(): lax.all_gather(feature_one, ('tensor', 'examples'), axis=0, tiled=True)]
    pallas_call x0 -> x2, Pallas kernels: none -> 44.8 us  [the longest x1 24.5 us: shards(): pl.pallas_call(functools.partial(exchange_kernel, n_tensor, n_core, own_r...]
    dot_general x8 -> x0, matrix products: 39.6 us -> none  [the longest x2 32 us: cross_product(): lax.dot_general(left, right, (((0,), (0,)), ((), ())), precision=lax.Prec...]
    unnamed x5 -> x2, local copies, waits for them, and re-layouts: 4.81 us -> 4 us
  transfers between devices with their start and end apart: 3 -> 0, of which waited for: 3 -> 0; matrix products, arithmetic and copies ran while one was open for 10% -> 0% of each run, Pallas kernels for 0% -> 0%
where the time goes in v1:
time: 49.7 us; the launch traced here: 49.4 us
  Pallas kernels  44.8 us (90%)
  local copies, waits for them, and re-layouts  4 us (8%)
  between operations  0.64 us (1%)
    pallas_call x1, Pallas kernels, shards(): pl.pallas_call(functools.partial(exchange_kernel, n_tensor, n_core, own_r...  24.5 us
    pallas_call x1, Pallas kernels, shards(): pl.pallas_call(functools.partial(gram_kernel, n_tensor, n_core, seq_len,...  20.3 us
    unnamed x2, local copies, waits for them, and re-layouts  4 us

profile of v1, /device:TPU:1, one launch (start us, length us, event | category | flops | bytes accessed | tf_op | source)
XLA Modules:
  0.0 49.4 jit_solution(15842339874383911427)
XLA Ops:
  0.6 1.7 %copy.12.b_au = bf16[1024,64]{1,0:T(8,128)(2,1)} copy(bf16[1024,64]{0,1:T(8,128)(2,1)} %param.12) | data formatting | bytes 262144 | tf_op args[4]
  2.4 2.3 %copy.13.b_ad = bf16[3584,64]{1,0:T(8,128)(2,1)} copy(bf16[3584,64]{0,1:T(8,128)(2,1)} %param.14) | data formatting | bytes 917504 | tf_op args[6]
  4.6 24.5 %project_and_gather.1 = f32[3,2,2,4,32,128]{5,4,3,2,1,0:T(8,128)} custom-call(bf16[256,1024]{1,0:T(8,128)(2,1)} %bitcast.10, bf16[256,3584]{1,0:T(8,128)(2,1)} %bitcast.8, bf16[256,3584]{1,0:T(8,128)(2,1)} %bitcast.9, bf16[256,1024]{1,0:T(8,128)(2,1)} %bitcast.11, bf16[1024,64]{1,0:T(8,128)(2,1)} %copy.12.b_au, bf16[3584,128]{1,0:T(8,128)(2,1)} %b_gu.1, ...), custom_call_target="tpu_custom_call" | custom-call | tf_op jit(solution)/shard_map/project_and_gather/pallas_call | solution.py:249
  29.1 20.3 %features_and_gram.1 = (f32[2,8192]{1,0:T(2,128)}, f32[4096,1024]{1,0:T(8,128)}, f32[2,8192]{1,0:T(2,128)}, f32[4096,1024]{1,0:T(8,128)}) custom-call(f32[3,512,128]{2,1,0:T(8,128)} %bitcast.7), custom_call_target="tpu_custom_call" | custom-call | tf_op jit(solution)/shard_map/features_and_gram/pallas_call | solution.py:275

commit v2 on v1

--- a/solution.py
+++ b/solution.py
@@ -9,6 +9,7 @@
 from jax.sharding import PartitionSpec as P
 
 LANES = 128
+TILE = 256
 MESH = pl.DeviceIdType.MESH
 VMEM_LIMIT = 56 * 1024 * 1024
 
@@ -48,7 +49,8 @@
         loads[i][0].wait()
         loads[i][1].wait()
         v, w = sources[i][2:]
-        return jnp.dot(v[...], w[...], preferred_element_type=jnp.float32)
+        dims = (((1,), (0 if i < 2 else 1,)), ((), ()))
+        return lax.dot_general(v[...], w[...], dims, preferred_element_type=jnp.float32)
 
     pair_copies = []
     for c in range(3):
@@ -136,15 +138,17 @@
 def features_of(grad_pair, act_tile, first, columns, seq_len, width_in):
     width_out = grad_pair.shape[1] // 2
     batch = grad_pair.shape[0] // seq_len
-    pick = lax.broadcasted_iota(jnp.int32, (width_out, columns), 0) - lax.broadcasted_iota(
-        jnp.int32, (width_out, columns), 1) // width_in
-    pick = jnp.where(pick == first, 1.0, 0.0).astype(jnp.bfloat16)
-    pick = jnp.concatenate([pick, pick], axis=0)
-    spread = jnp.dot(grad_pair, pick, preferred_element_type=jnp.float32)
+    tile = min(TILE, columns)
     pieces = []
-    for start in range(0, columns, LANES):
-        piece = spread[:, start:start + LANES] * act_tile
-        pieces.append(piece.reshape(seq_len, batch, LANES).sum(axis=0))
+    for start in range(0, columns, tile):
+        pick = lax.broadcasted_iota(jnp.int32, (width_out, tile), 0) - (
+            lax.broadcasted_iota(jnp.int32, (width_out, tile), 1) + start) // width_in
+        pick = jnp.where(pick == first, 1.0, 0.0).astype(jnp.bfloat16)
+        pick = jnp.concatenate([pick, pick], axis=0)
+        spread = jnp.dot(grad_pair[...], pick, preferred_element_type=jnp.float32)
+        for part in range(0, tile, LANES):
+            piece = spread[:, part:part + LANES] * act_tile[...]
+            pieces.append(piece.reshape(seq_len, batch, LANES).sum(axis=0))
     return jnp.concatenate(pieces, axis=1)
 
 
@@ -197,7 +201,7 @@
         own_act[...] = jnp.concatenate(acts, axis=0)
 
         columns = a_cols * width_in
-        value = features_of(grad_pair[...], act_tile[...], t * a_cols, columns, seq_len, width_in)
+        value = features_of(grad_pair, act_tile, t * a_cols, columns, seq_len, width_in)
         high, low = split_lanes(value * (1.0 / total_examples))
         right[0:batch] = high
         right[batch:2 * batch] = low
@@ -205,10 +209,6 @@
 
         def step(i, carry):
             slot = lax.rem(i + layer * n_blocks, slots)
-            value = features_of(grad_pair[...], act_tile[...], e * a_rows + i * a_block, block, seq_len, width_in)
-            high, low = split_lanes(value)
-            left = jnp.concatenate([high, high, low], axis=0)
-            product = lax.dot_general(left, right[...], (((0,), (0,)), ((), ())), preferred_element_type=jnp.float32)
 
             def wait():
                 pltpu.make_async_copy(held.at[slot], gram.at[pl.ds(0, block)], gram_sem.at[slot]).wait()
@@ -217,10 +217,16 @@
                 pl.when(i >= slots)(wait)
             else:
                 wait()
-            held[slot] = product
+            value = features_of(grad_pair, act_tile, e * a_rows + i * a_block, block, seq_len, width_in)
+            high, low = split_lanes(value)
+            left = jnp.concatenate([high, high, low], axis=0)
+            for start in range(0, columns, TILE):
+                held[slot, :, start:start + TILE] = lax.dot_general(
+                    left, right[:, start:start + TILE], (((0,), (0,)), ((), ())),
+                    preferred_element_type=jnp.float32)
             pltpu.make_async_copy(
                 held.at[slot], gram.at[pl.ds(pl.multiple_of(i * block, block), block)], gram_sem.at[slot]).start()
-            value = features_of(own_grad[...], own_act[...], i * a_part, feat_part, seq_len, width_in)
+            value = features_of(own_grad, own_act, i * a_part, feat_part, seq_len, width_in)
             own_feat[layer, :, pl.ds(pl.multiple_of(i * feat_part, feat_part), feat_part)] = value
             return carry
 
@@ -237,7 +243,7 @@
     ex_local, seq_len = act_up.shape[0], act_up.shape[1]
     token_rows = ex_local * seq_len
     acts = [a.reshape(token_rows, a.shape[2]) for a in (act_up, grad_up, act_down, grad_down)]
-    bases = [b_au, b_gu, b_ad, b_gd]
+    bases = [b_au.T, b_gu, b_ad.T, b_gd]
     width_in, width_out = b_au.shape[1], b_gu.shape[1]
     own_rows = token_rows // n_tensor
     owned = own_rows // seq_len

time: 49.7 us -> 42.7 us (0.86)
  local copies, waits for them, and re-layouts: 4 us -> 0 us
  Pallas kernels: 44.8 us -> 41.9 us
    unnamed x2 -> x0, local copies, waits for them, and re-layouts: 4 us -> none
    pallas_call x1, Pallas kernels: 20.3 us -> 16.8 us  [shards(): pl.pallas_call(functools.partial(gram_kernel, n_tensor, n_core, seq_len,...]
    pallas_call x1, Pallas kernels: 24.5 us -> 25.1 us  [shards(): pl.pallas_call(functools.partial(exchange_kernel, n_tensor, n_core, own_r...]
where the time goes in v2:
time: 42.7 us; the launch traced here: 42.6 us
  Pallas kernels  41.9 us (98%)
  between operations  0.64 us (1%)
    pallas_call x1, Pallas kernels, shards(): pl.pallas_call(functools.partial(exchange_kernel, n_tensor, n_core, own_r...  25.1 us
    pallas_call x1, Pallas kernels, shards(): pl.pallas_call(functools.partial(gram_kernel, n_tensor, n_core, seq_len,...  16.8 us

profile of v2, /device:TPU:1, one launch (start us, length us, event | category | flops | bytes accessed | tf_op | source)
XLA Modules:
  0.0 42.6 jit_solution(7347202509195839722)
XLA Ops:
  0.6 25.1 %project_and_gather.1 = f32[3,2,2,4,32,128]{5,4,3,2,1,0:T(8,128)} custom-call(bf16[256,1024]{1,0:T(8,128)(2,1)} %bitcast.12, bf16[256,3584]{1,0:T(8,128)(2,1)} %bitcast.10, bf16[256,3584]{1,0:T(8,128)(2,1)} %bitcast.11, bf16[256,1024]{1,0:T(8,128)(2,1)} %bitcast.13, bf16[64,1024]{1,0:T(8,128)(2,1)} %bitcast.15, bf16[3584,128]{1,0:T(8,128)(2,1)} %b_gu.1, ...), custom_call_target="tpu_custom_call" | custom-call | tf_op jit(solution)/shard_map/project_and_gather/pallas_call | solution.py:255
  25.8 16.8 %features_and_gram.1 = (f32[2,8192]{1,0:T(2,128)}, f32[4096,1024]{1,0:T(8,128)}, f32[2,8192]{1,0:T(2,128)}, f32[4096,1024]{1,0:T(8,128)}) custom-call(f32[3,512,128]{2,1,0:T(8,128)} %bitcast.9), custom_call_target="tpu_custom_call" | custom-call | tf_op jit(solution)/shard_map/features_and_gram/pallas_call | solution.py:281

commit v3 on v2

--- a/solution.py
+++ b/solution.py
@@ -10,6 +10,7 @@
 
 LANES = 128
 TILE = 256
+GROUPS = ((0, 1), (1, 2), (2, 3))
 MESH = pl.DeviceIdType.MESH
 VMEM_LIMIT = 56 * 1024 * 1024
 
@@ -53,72 +54,74 @@
         return lax.dot_general(v[...], w[...], dims, preferred_element_type=jnp.float32)
 
     pair_copies = []
-    for c in range(3):
-        value = product(c) if c < 2 else jnp.concatenate([product(2), product(3)], axis=1)
-        for owner in range(n_tensor):
-            part[c, owner % 2, owner // 2] = value[owner * own_rows:(owner + 1) * own_rows]
-        if c == 0:
+    for g, (lo, hi) in enumerate(GROUPS):
+        for c in range(lo, hi):
+            value = product(c) if c < 2 else jnp.concatenate([product(2), product(3)], axis=1)
+            for owner in range(n_tensor):
+                part[c, owner % 2, owner // 2] = value[owner * own_rows:(owner + 1) * own_rows]
+        if g == 0:
             pl.semaphore_wait(barrier, 1 + (n_line - 1) + (n_core - 1))
         copy = pltpu.make_async_remote_copy(
-            src_ref=part.at[c, 1 - y], dst_ref=pair_in.at[c], send_sem=pair_send.at[c], recv_sem=pair_recv.at[c],
-            device_id=pair, device_id_type=MESH)
+            src_ref=part.at[lo:hi, 1 - y], dst_ref=pair_in.at[lo:hi], send_sem=pair_send.at[g],
+            recv_sem=pair_recv.at[g], device_id=pair, device_id_type=MESH)
         copy.start()
         pair_copies.append(copy)
 
     line_copies = []
-    for c in range(3):
-        pair_copies[c].wait_recv()
-        pair_in[c] = pair_in[c] + part[c, y]
+    for g, (lo, hi) in enumerate(GROUPS):
+        pair_copies[g].wait_recv()
+        pair_in[lo:hi] = pair_in[lo:hi] + part[lo:hi, y]
         copies = []
         for step in range(1, n_line):
             copy = pltpu.make_async_remote_copy(
-                src_ref=pair_in.at[c, lax.rem(z + step, n_line)], dst_ref=line_in.at[c, step - 1],
-                send_sem=line_send.at[c, step - 1], recv_sem=line_recv.at[c, step - 1],
+                src_ref=pair_in.at[lo:hi, lax.rem(z + step, n_line)], dst_ref=line_in.at[lo:hi, step - 1],
+                send_sem=line_send.at[g, step - 1], recv_sem=line_recv.at[g, step - 1],
                 device_id=line(step), device_id_type=MESH)
             copy.start()
             copies.append(copy)
         line_copies.append(copies)
 
     gat_copies = []
-    for c in range(3):
-        total = pair_in[c, z]
+    for g, (lo, hi) in enumerate(GROUPS):
+        total = pair_in[lo:hi, z]
         for step in range(1, n_line):
-            line_copies[c][step - 1].wait_recv()
-            total = total + line_in[c, step - 1]
-        whole[c, e, y, z] = total
+            line_copies[g][step - 1].wait_recv()
+            total = total + line_in[lo:hi, step - 1]
+        whole[lo:hi, e, y, z] = total
         copies = []
         for step in range(1, n_line):
             copy = pltpu.make_async_remote_copy(
-                src_ref=whole.at[c, e, y, z], dst_ref=whole.at[c, e, y, z],
-                send_sem=gat_send.at[c, step - 1], recv_sem=gat_recv.at[c, step - 1],
+                src_ref=whole.at[lo:hi, e, y, z], dst_ref=whole.at[lo:hi, e, y, z],
+                send_sem=gat_send.at[g, step - 1], recv_sem=gat_recv.at[g, step - 1],
                 device_id=line(step), device_id_type=MESH)
             copy.start()
             copies.append(copy)
         gat_copies.append(copies)
 
-    back_copies, core_copies, outs = [], [], []
-
-    def to_cores(c, side, half):
+    back_copies, core_copies = [], []
+
+    def to_cores(g, side, half):
+        lo, hi = GROUPS[g]
         for step in range(1, n_core):
             copy = pltpu.make_async_remote_copy(
-                src_ref=whole.at[c, e, half], dst_ref=whole.at[c, e, half],
-                send_sem=core_send.at[c, side, step - 1], recv_sem=core_recv.at[c, side, step - 1],
+                src_ref=whole.at[lo:hi, e, half], dst_ref=whole.at[lo:hi, e, half],
+                send_sem=core_send.at[g, side, step - 1], recv_sem=core_recv.at[g, side, step - 1],
                 device_id={"examples": lax.rem(e + step, n_core)}, device_id_type=MESH)
             copy.start()
             core_copies.append(copy)
 
-    for c in range(3):
-        for copy in gat_copies[c]:
+    for g, (lo, hi) in enumerate(GROUPS):
+        for copy in gat_copies[g]:
             copy.wait_recv()
         copy = pltpu.make_async_remote_copy(
-            src_ref=whole.at[c, e, y], dst_ref=whole.at[c, e, y], send_sem=back_send.at[c], recv_sem=back_recv.at[c],
-            device_id=pair, device_id_type=MESH)
+            src_ref=whole.at[lo:hi, e, y], dst_ref=whole.at[lo:hi, e, y], send_sem=back_send.at[g],
+            recv_sem=back_recv.at[g], device_id=pair, device_id_type=MESH)
         copy.start()
         back_copies.append(copy)
-        to_cores(c, 0, y)
-    for c in range(3):
-        back_copies[c].wait_recv()
-        to_cores(c, 1, 1 - y)
+        to_cores(g, 0, y)
+    for g in range(len(GROUPS)):
+        back_copies[g].wait_recv()
+        to_cores(g, 1, 1 - y)
     for copy in core_copies:
         copy.wait_recv()
     out = pltpu.make_async_copy(whole, gathered, out_sem)
@@ -154,7 +157,7 @@
 
 def gram_kernel(n_tensor, n_core, seq_len, width_in, block, slots,
                 gathered, feat_up, gram_up, feat_down, gram_down,
-                rows, grad_pair, act_tile, own_grad, own_act, right, own_feat, held, load_sem, feat_sem, gram_sem):
+                rows, grad_pair, act_tile, own_grad, own_act, right, left_even, left_odd, own_feat, held, load_sem, feat_sem, gram_sem):
     t = lax.axis_index("tensor")
     e = lax.axis_index("examples")
     n_line = n_tensor // 2
@@ -205,9 +208,20 @@
         high, low = split_lanes(value * (1.0 / total_examples))
         right[0:batch] = high
         right[batch:2 * batch] = low
-        right[2 * batch:] = high
-
-        def step(i, carry):
+        right[2 * batch:3 * batch] = high
+        if right.shape[0] > 3 * batch:
+            right[3 * batch:] = jnp.zeros((right.shape[0] - 3 * batch, columns), jnp.bfloat16)
+
+        def prepare(i, target):
+            value = features_of(grad_pair, act_tile, e * a_rows + i * a_block, block, seq_len, width_in)
+            high, low = split_lanes(value)
+            high, low = high.astype(jnp.float32), low.astype(jnp.float32)
+            left = [high, high, low]
+            if right.shape[0] > 3 * batch:
+                left.append(jnp.zeros((right.shape[0] - 3 * batch, block), jnp.float32))
+            target[...] = jnp.concatenate(left, axis=0).T.astype(jnp.bfloat16)
+
+        def step(i, current, following):
             slot = lax.rem(i + layer * n_blocks, slots)
 
             def wait():
@@ -217,20 +231,22 @@
                 pl.when(i >= slots)(wait)
             else:
                 wait()
-            value = features_of(grad_pair, act_tile, e * a_rows + i * a_block, block, seq_len, width_in)
-            high, low = split_lanes(value)
-            left = jnp.concatenate([high, high, low], axis=0)
             for start in range(0, columns, TILE):
-                held[slot, :, start:start + TILE] = lax.dot_general(
-                    left, right[:, start:start + TILE], (((0,), (0,)), ((), ())),
-                    preferred_element_type=jnp.float32)
+                held[slot, :, start:start + TILE] = jnp.dot(
+                    current[...], right[:, start:start + TILE], preferred_element_type=jnp.float32)
+            prepare(lax.rem(i + 1, n_blocks), following)
+            value = features_of(own_grad, own_act, i * a_part, feat_part, seq_len, width_in)
+            own_feat[layer, :, pl.ds(pl.multiple_of(i * feat_part, feat_part), feat_part)] = value
             pltpu.make_async_copy(
                 held.at[slot], gram.at[pl.ds(pl.multiple_of(i * block, block), block)], gram_sem.at[slot]).start()
-            value = features_of(own_grad, own_act, i * a_part, feat_part, seq_len, width_in)
-            own_feat[layer, :, pl.ds(pl.multiple_of(i * feat_part, feat_part), feat_part)] = value
+
+        def two_steps(i, carry):
+            step(2 * i, left_even, left_odd)
+            step(2 * i + 1, left_odd, left_even)
             return carry
 
-        lax.fori_loop(0, n_blocks, step, 0)
+        prepare(0, left_even)
+        lax.fori_loop(0, n_blocks // 2, two_steps, 0)
         pltpu.make_async_copy(own_feat.at[layer], feat, feat_sem.at[layer]).start()
 
     for slot in range(slots):
@@ -276,6 +292,7 @@
     feat = width_in * width_out
     row_width, col_width = feat // n_core, feat // n_tensor
     block, slots = 512, 4
+    depth = -(-3 * batch // LANES) * LANES
     shape = jax.ShapeDtypeStruct
     bf16 = jnp.bfloat16
     feature_one, gram_one, feature_two, gram_two = pl.pallas_call(
@@ -289,7 +306,9 @@
             pltpu.VMEM((tokens, LANES), f32),
             pltpu.VMEM((own_rows, 2 * width_out), bf16),
             pltpu.VMEM((own_rows, LANES), f32),
-            pltpu.VMEM((3 * batch, col_width), bf16),
+            pltpu.VMEM((depth, col_width), bf16),
+            pltpu.VMEM((block, depth), bf16),
+            pltpu.VMEM((block, depth), bf16),
             pltpu.VMEM((2, owned, feat), f32),
             pltpu.VMEM((slots, block, col_width), f32),
             dma, dma((2,)), dma((slots,)),

time: 42.7 us -> 40.5 us (0.948)
  Pallas kernels: 41.9 us -> 39.7 us
    pallas_call x1, Pallas kernels: 16.8 us -> 14.5 us  [shards(): pl.pallas_call(functools.partial(gram_kernel, n_tensor, n_core, seq_len,...]
where the time goes in v3:
time: 40.5 us; the launch traced here: 40.3 us
  Pallas kernels  39.7 us (98%)
  between operations  0.64 us (2%)
    pallas_call x1, Pallas kernels, shards(): pl.pallas_call(functools.partial(exchange_kernel, n_tensor, n_core, own_r...  25.1 us
    pallas_call x1, Pallas kernels, shards(): pl.pallas_call(functools.partial(gram_kernel, n_tensor, n_core, seq_len,...  14.5 us

profile of v3, /device:TPU:1, one launch (start us, length us, event | category | flops | bytes accessed | tf_op | source)
XLA Modules:
  0.0 40.3 jit_solution(6598181817304341362)
XLA Ops:
  0.6 25.1 %project_and_gather.1 = f32[3,2,2,4,32,128]{5,4,3,2,1,0:T(8,128)} custom-call(bf16[256,1024]{1,0:T(8,128)(2,1)} %bitcast.12, bf16[256,3584]{1,0:T(8,128)(2,1)} %bitcast.10, bf16[256,3584]{1,0:T(8,128)(2,1)} %bitcast.11, bf16[256,1024]{1,0:T(8,128)(2,1)} %bitcast.13, bf16[64,1024]{1,0:T(8,128)(2,1)} %bitcast.15, bf16[3584,128]{1,0:T(8,128)(2,1)} %b_gu.1, ...), custom_call_target="tpu_custom_call" | custom-call | tf_op jit(solution)/shard_map/project_and_gather/pallas_call | solution.py:271
  25.8 14.5 %features_and_gram.1 = (f32[2,8192]{1,0:T(2,128)}, f32[4096,1024]{1,0:T(8,128)}, f32[2,8192]{1,0:T(2,128)}, f32[4096,1024]{1,0:T(8,128)}) custom-call(f32[3,512,128]{2,1,0:T(8,128)} %bitcast.9), custom_call_target="tpu_custom_call" | custom-call | tf_op jit(solution)/shard_map/features_and_gram/pallas_call | solution.py:298

commit v4 on v3

--- a/solution.py
+++ b/solution.py
@@ -98,7 +98,13 @@
             copies.append(copy)
         gat_copies.append(copies)
 
-    back_copies, core_copies = [], []
+    back_copies, core_copies, outs = [], {}, []
+
+    def write_out(c, step):
+        source = lax.rem(e + n_core - step, n_core)
+        out = pltpu.make_async_copy(whole.at[c, source], gathered.at[c, source], out_sem.at[c, step])
+        out.start()
+        outs.append(out)
 
     def to_cores(g, side, half):
         lo, hi = GROUPS[g]
@@ -108,7 +114,7 @@
                 send_sem=core_send.at[g, side, step - 1], recv_sem=core_recv.at[g, side, step - 1],
                 device_id={"examples": lax.rem(e + step, n_core)}, device_id_type=MESH)
             copy.start()
-            core_copies.append(copy)
+            core_copies[(g, side, step)] = copy
 
     for g, (lo, hi) in enumerate(GROUPS):
         for copy in gat_copies[g]:
@@ -119,15 +125,21 @@
         copy.start()
         back_copies.append(copy)
         to_cores(g, 0, y)
-    for g in range(len(GROUPS)):
+    for g, (lo, hi) in enumerate(GROUPS):
         back_copies[g].wait_recv()
         to_cores(g, 1, 1 - y)
-    for copy in core_copies:
-        copy.wait_recv()
-    out = pltpu.make_async_copy(whole, gathered, out_sem)
-    out.start()
-    out.wait()
-    for copies in [pair_copies, back_copies, core_copies] + line_copies + gat_copies:
+        for c in range(lo, hi):
+            write_out(c, 0)
+    for g, (lo, hi) in enumerate(GROUPS):
+        for side in range(2):
+            for step in range(1, n_core):
+                core_copies[(g, side, step)].wait_recv()
+        for c in range(lo, hi):
+            for step in range(1, n_core):
+                write_out(c, step)
+    for out in outs:
+        out.wait()
+    for copies in [pair_copies, back_copies, list(core_copies.values())] + line_copies + gat_copies:
         for copy in copies:
             copy.wait_send()
 
@@ -143,10 +155,10 @@
     batch = grad_pair.shape[0] // seq_len
     tile = min(TILE, columns)
     pieces = []
+    offset = lax.broadcasted_iota(jnp.int32, (width_out, tile), 0) - lax.broadcasted_iota(
+        jnp.int32, (width_out, tile), 1) // width_in
     for start in range(0, columns, tile):
-        pick = lax.broadcasted_iota(jnp.int32, (width_out, tile), 0) - (
-            lax.broadcasted_iota(jnp.int32, (width_out, tile), 1) + start) // width_in
-        pick = jnp.where(pick == first, 1.0, 0.0).astype(jnp.bfloat16)
+        pick = jnp.where(offset == first + start // width_in, 1.0, 0.0).astype(jnp.bfloat16)
         pick = jnp.concatenate([pick, pick], axis=0)
         spread = jnp.dot(grad_pair[...], pick, preferred_element_type=jnp.float32)
         for part in range(0, tile, LANES):
@@ -174,12 +186,14 @@
     own_at = pl.multiple_of((e * n_tensor + (t % 2) * n_line + t // 2) * (own * seq_len), own * seq_len)
     scale = 1.0 / math.sqrt(seq_len)
 
-    load = pltpu.make_async_copy(gathered, rows, load_sem)
-    load.start()
-    load.wait()
+    loads = [pltpu.make_async_copy(gathered.at[c], rows.at[c], load_sem.at[c]) for c in range(3)]
+    for c in (2, 1, 0):
+        loads[c].start()
+    loads[2].wait()
 
     for layer, (gram, feat) in enumerate(((gram_up, feat_up), (gram_down, feat_down))):
         chunk = 1 - layer
+        loads[chunk].wait()
         lane = lax.broadcasted_iota(jnp.int32, (batch, LANES), 1)
         for s in range(seq_len):
             at = pl.ds(s * batch, batch)
@@ -278,7 +292,7 @@
             pltpu.VMEM((3, n_line, own_rows, LANES), f32),
             pltpu.VMEM((3, steps, own_rows, LANES), f32),
             pltpu.VMEM((3, n_core, 2, n_line, own_rows, LANES), f32),
-            dma((8,)), dma,
+            dma((8,)), dma((3, n_core)),
             dma((3,)), dma((3,)), dma((3, steps)), dma((3, steps)), dma((3, steps)), dma((3, steps)),
             dma((3,)), dma((3,)), dma((3, 2, n_core - 1)), dma((3, 2, n_core - 1)),
         ],
@@ -311,7 +325,7 @@
             pltpu.VMEM((block, depth), bf16),
             pltpu.VMEM((2, owned, feat), f32),
             pltpu.VMEM((slots, block, col_width), f32),
-            dma, dma((2,)), dma((slots,)),
+            dma((3,)), dma((2,)), dma((slots,)),
         ],
         compiler_params=pltpu.CompilerParams(vmem_limit_bytes=VMEM_LIMIT),
         name="features_and_gram",

time: 40.5 us -> 40.1 us (level)
  no operation moved by 1% of the time
where the time goes in v4:
time: 40.1 us; the launch traced here: 39.9 us
  Pallas kernels  39.3 us (98%)
  between operations  0.64 us (2%)
    pallas_call x1, Pallas kernels, shards(): pl.pallas_call(functools.partial(exchange_kernel, n_tensor, n_core, own_r...  24.9 us
    pallas_call x1, Pallas kernels, shards(): pl.pallas_call(functools.partial(gram_kernel, n_tensor, n_core, seq_len,...  14.4 us

profile of v4, /device:TPU:1, one launch (start us, length us, event | category | flops | bytes accessed | tf_op | source)
XLA Modules:
  0.0 39.9 jit_solution(2402195431312676549)
XLA Ops:
  0.6 24.9 %project_and_gather.1 = f32[3,2,2,4,32,128]{5,4,3,2,1,0:T(8,128)} custom-call(bf16[256,1024]{1,0:T(8,128)(2,1)} %bitcast.12, bf16[256,3584]{1,0:T(8,128)(2,1)} %bitcast.10, bf16[256,3584]{1,0:T(8,128)(2,1)} %bitcast.11, bf16[256,1024]{1,0:T(8,128)(2,1)} %bitcast.13, bf16[64,1024]{1,0:T(8,128)(2,1)} %bitcast.15, bf16[3584,128]{1,0:T(8,128)(2,1)} %b_gu.1, ...), custom_call_target="tpu_custom_call" | custom-call | tf_op jit(solution)/shard_map/project_and_gather/pallas_call | solution.py:285
  25.6 14.4 %features_and_gram.1 = (f32[2,8192]{1,0:T(2,128)}, f32[4096,1024]{1,0:T(8,128)}, f32[2,8192]{1,0:T(2,128)}, f32[4096,1024]{1,0:T(8,128)}) custom-call(f32[3,512,128]{2,1,0:T(8,128)} %bitcast.9), custom_call_target="tpu_custom_call" | custom-call | tf_op jit(solution)/shard_map/features_and_gram/pallas_call | solution.py:312
